TPU v7x, 32 devices: a whole 2x2x4 slice. The times are simulated.
32 devices in a mesh: head: 4 (over y, core), seq: 8 (over z, x).
Axes of the slice: x: 2, y: 2, z: 4, core: 2. Of those that a mesh axis runs over, the one named last changes fastest.
Arguments:
- query_rows: bfloat16 [8192, 1024], P(('seq', 'head')), may hold values from -0.5 to 0.5
- key_rows: bfloat16 [8192, 1024], P(('seq', 'head')), may hold values from -0.5 to 0.5
- value_rows: bfloat16 [8192, 1024], P(('seq', 'head')), may hold values from -0.5 to 0.5
- grad_rows: bfloat16 [8192, 1024], P(('seq', 'head')), may hold values from -0.5 to 0.5
Outputs:
- attended: bfloat16 [8192, 1024], P(('seq', 'head'))
- grad_query: bfloat16 [8192, 1024], P(('seq', 'head'))
- grad_key: bfloat16 [8192, 1024], P(('seq', 'head'))
- grad_value: bfloat16 [8192, 1024], P(('seq', 'head'))
All inputs are finite; a program needn't handle non-finite values.
Results may differ from a plain program's by a relative error of at most 0.0051.
Values may be sent and summed in bfloat16 or wider, within the bound.
A program may use at most 64 MiB of HBM per device.

v0:
```python
import jax
import jax.numpy as jnp
from jax import lax
from jax.sharding import PartitionSpec as P

HEAD_DIM = 128


def split_heads(rows):
    count = rows.shape[0]
    return jnp.transpose(rows.reshape(count, rows.shape[1] // HEAD_DIM, HEAD_DIM), (1, 0, 2))


def join_heads(blocks):
    return jnp.transpose(blocks, (1, 0, 2)).reshape(blocks.shape[1], blocks.shape[0] * HEAD_DIM)


def one_head(items):
    query, keyset, valueset, cograd, prefix, suffix = items
    count = query.shape[0]
    rowpos = lax.broadcasted_iota(jnp.int32, (count, count), 0)
    colpos = lax.broadcasted_iota(jnp.int32, (count, count), 1)
    causal = colpos <= rowpos
    prefix16 = prefix.astype(jnp.bfloat16)
    suffix16 = suffix.astype(jnp.bfloat16)
    raw_scores = jnp.einsum("td,sd->ts", query, keyset, preferred_element_type=jnp.float32)
    scores = jnp.where(causal, raw_scores, 0.0).astype(jnp.bfloat16)
    attended = jnp.dot(scores, valueset, preferred_element_type=jnp.float32)
    attended = attended + jnp.dot(query, prefix16, preferred_element_type=jnp.float32)
    raw_dprob = jnp.einsum("td,sd->ts", cograd, valueset, preferred_element_type=jnp.float32)
    dprob = jnp.where(causal, raw_dprob, 0.0).astype(jnp.bfloat16)
    grad_query = jnp.dot(dprob, keyset, preferred_element_type=jnp.float32)
    grad_query = grad_query + jnp.einsum(
        "td,ed->te", cograd, prefix16, preferred_element_type=jnp.float32
    )
    grad_key = jnp.einsum("ts,td->sd", dprob, query, preferred_element_type=jnp.float32)
    grad_key = grad_key + jnp.einsum(
        "se,de->sd", valueset, suffix16, preferred_element_type=jnp.float32
    )
    grad_value = jnp.einsum("ts,te->se", scores, cograd, preferred_element_type=jnp.float32)
    grad_value = grad_value + jnp.dot(keyset, suffix16, preferred_element_type=jnp.float32)
    return (
        attended.astype(jnp.bfloat16),
        grad_query.astype(jnp.bfloat16),
        grad_key.astype(jnp.bfloat16),
        grad_value.astype(jnp.bfloat16),
    )


def per_device(query_rows, key_rows, value_rows, grad_rows):
    query_all, key_all, value_all, grad_all = (
        lax.all_to_all(query_rows, "head", split_axis=1, concat_axis=0, tiled=True),
        lax.all_to_all(key_rows, "head", split_axis=1, concat_axis=0, tiled=True),
        lax.all_to_all(value_rows, "head", split_axis=1, concat_axis=0, tiled=True),
        lax.all_to_all(grad_rows, "head", split_axis=1, concat_axis=0, tiled=True),
    )
    query = split_heads(query_all)
    keyset = split_heads(key_all)
    valueset = split_heads(value_all)
    cograd = split_heads(grad_all)
    state = jnp.einsum("htd,hte->hde", keyset, valueset, preferred_element_type=jnp.float32)
    qgrad = jnp.einsum("htd,hte->hde", query, cograd, preferred_element_type=jnp.float32)
    myself = lax.axis_index("seq")
    state_piece = lax.all_gather(state[None], "seq", axis=0, tiled=True)
    qgrad_piece = lax.all_gather(qgrad[None], "seq", axis=0, tiled=True)
    position = jnp.arange(state_piece.shape[0], dtype=jnp.int32)
    before = (position < myself).astype(jnp.float32)[:, None, None, None]
    after = (position > myself).astype(jnp.float32)[:, None, None, None]
    prefix = jnp.sum(state_piece * before, axis=0)
    suffix = jnp.sum(qgrad_piece * after, axis=0)
    attended, grad_query, grad_key, grad_value = lax.map(
        one_head, (query, keyset, valueset, cograd, prefix, suffix)
    )
    results = (
        lax.all_to_all(join_heads(attended), "head", split_axis=0, concat_axis=1, tiled=True),
        lax.all_to_all(join_heads(grad_query), "head", split_axis=0, concat_axis=1, tiled=True),
        lax.all_to_all(join_heads(grad_key), "head", split_axis=0, concat_axis=1, tiled=True),
        lax.all_to_all(join_heads(grad_value), "head", split_axis=0, concat_axis=1, tiled=True),
    )
    return (results[0], results[1], results[2], results[3])


def solution(mesh):
    placed = (
        P(("seq", "head"), None),
        P(("seq", "head"), None),
        P(("seq", "head"), None),
        P(("seq", "head"), None),
    )
    return jax.shard_map(
        per_device,
        mesh=mesh,
        in_specs=placed,
        out_specs=(
            P(("seq", "head"), None),
            P(("seq", "head"), None),
            P(("seq", "head"), None),
            P(("seq", "head"), None),
        ),
        check_vma=False,
    )
```

profile of v0, /device:TPU:1, one launch (start us, length us, event | category | flops | bytes accessed | tf_op | source)
XLA Modules:
  0.0 192.3 jit_solution(12298459079657299575)
XLA Ops:
  7.2 2.1 %copy.46 = bf16[256,1024]{0,1:T(8,128)(2,1)} copy(bf16[256,1024]{1,0:T(8,128)(2,1)} %param.7) | data formatting | bytes 1048576 | tf_op args[1]
  9.3 4.3 %all-to-all-start.1 = ((bf16[256,4,256]{0,2,1:T(8,128)(2,1)}), bf16[256,4,256]{0,2,1:T(8,128)(2,1)S(1)}, u32[]{:S(2)}, u32[]{:S(2)}) async-start(bf16[256,4,256]{0,2,1:T(8,128)(2,1)} %bitcast.13), calls=%async_computation.1 | async-start | bytes 1048576 | tf_op jit(solution)/shard_map/all_to_all | solution.py:53
  13.6 0.8 copy.77
  14.4 7.0 %all-to-all-done.1 = bf16[256,4,256]{0,2,1:T(8,128)(2,1)S(1)} async-done(((bf16[256,4,256]{0,2,1:T(8,128)(2,1)}), bf16[256,4,256]{0,2,1:T(8,128)(2,1)S(1)}, u32[]{:S(2)}, u32[]{:S(2)}) %all-to-all-start.1) | async-done | bytes 524320 | tf_op jit(solution)/shard_map/all_to_all | solution.py:53
  21.4 4.5 %all-to-all-start.2 = ((bf16[256,4,256]{2,0,1:T(8,128)(2,1)}), bf16[256,4,256]{2,0,1:T(8,128)(2,1)S(1)}, u32[]{:S(2)}, u32[]{:S(2)}) async-start(bf16[256,4,256]{2,0,1:T(8,128)(2,1)} %bitcast.105), calls=%async_computation.2 | async-start | bytes 1048576 | tf_op jit(solution)/shard_map/all_to_all | solution.py:54
  25.9 0.4 copy.47
  26.3 0.4 reshape.71
  26.6 7.2 %all-to-all-done.2 = bf16[256,4,256]{2,0,1:T(8,128)(2,1)S(1)} async-done(((bf16[256,4,256]{2,0,1:T(8,128)(2,1)}), bf16[256,4,256]{2,0,1:T(8,128)(2,1)S(1)}, u32[]{:S(2)}, u32[]{:S(2)}) %all-to-all-start.2) | async-done | bytes 524320 | tf_op jit(solution)/shard_map/all_to_all | solution.py:54
  34.0 0.9 fusion.56
  34.9 1.0 copy.44
  35.9 4.3 %all-to-all-start = ((bf16[256,4,256]{0,2,1:T(8,128)(2,1)}), bf16[256,4,256]{0,2,1:T(8,128)(2,1)S(1)}, u32[]{:S(2)}, u32[]{:S(2)}) async-start(bf16[256,4,256]{0,2,1:T(8,128)(2,1)} %bitcast.10), calls=%async_computation | async-start | bytes 1048576 | tf_op jit(solution)/shard_map/all_to_all | solution.py:52
  40.3 0.8 copy.76
  41.1 7.3 %all-to-all-done = bf16[256,4,256]{0,2,1:T(8,128)(2,1)S(1)} async-done(((bf16[256,4,256]{0,2,1:T(8,128)(2,1)}), bf16[256,4,256]{0,2,1:T(8,128)(2,1)S(1)}, u32[]{:S(2)}, u32[]{:S(2)}) %all-to-all-start) | async-done | bytes 524320 | tf_op jit(solution)/shard_map/all_to_all | solution.py:52
  48.3 4.2 %all-to-all-start.3 = ((bf16[256,4,256]{2,0,1:T(8,128)(2,1)}), bf16[256,4,256]{2,0,1:T(8,128)(2,1)S(1)}, u32[]{:S(2)}, u32[]{:S(2)}) async-start(bf16[256,4,256]{2,0,1:T(8,128)(2,1)} %bitcast.104), calls=%async_computation.3 | async-start | bytes 1048576 | tf_op jit(solution)/shard_map/all_to_all | solution.py:55
  52.6 0.4 copy.45
  53.0 0.4 reshape.70
  53.3 7.2 %all-to-all-done.3 = bf16[256,4,256]{2,0,1:T(8,128)(2,1)S(1)} async-done(((bf16[256,4,256]{2,0,1:T(8,128)(2,1)}), bf16[256,4,256]{2,0,1:T(8,128)(2,1)S(1)}, u32[]{:S(2)}, u32[]{:S(2)}) %all-to-all-start.3) | async-done | bytes 524320 | tf_op jit(solution)/shard_map/all_to_all | solution.py:55
  60.7 1.0 fusion.58
  61.9 13.6 %all-gather.5.cloned.1.call-done = f32[16,128,128]{2,1,0:T(8,128)} async-done(((f32[2,128,128]{2,1,0:T(8,128)}), f32[16,128,128]{2,1,0:T(8,128)}) %all-gather.5.cloned.1.call-update) | async-done | bytes 1048592 | tf_op jit(solution)/shard_map/all_gather | solution.py:64
  75.4 1.4 multiply_reduce_fusion.1
  76.8 39.7 %all-gather.7.cloned.1.call-done = f32[16,128,128]{2,1,0:T(8,128)} async-done(((f32[2,128,128]{2,1,0:T(8,128)}), f32[16,128,128]{2,1,0:T(8,128)}) %all-gather.7.cloned.1.call-update) | async-done | bytes 1048592 | tf_op jit(solution)/shard_map/all_gather | solution.py:65
  116.5 1.4 multiply_reduce_fusion
  117.9 13.6 %while.16 = (s32[]{:T(128)}, bf16[2,1024,128]{2,1,0:T(8,128)(2,1)}, bf16[2,1024,128]{2,1,0:T(8,128)(2,1)}, bf16[2,1024,128]{2,1,0:T(8,128)(2,1)S(1)}, bf16[2,102...) while((s32[]{:T(128)}, bf16[2,1024,128]{2,1,0:T(8,128)(2,1)}, ...), condition=%wide.region_3.4_spmd, body=%wide.region_2.3_spmd.sunk | while | flops 1752170496 | bytes 29499644 | solution.py:71
  117.9 0.8 select_convert_fusion.5
  118.6 0.7 fusion.116
  119.4 0.7 fusion.114
  120.1 0.3 copy-done.5
  121.0 0.8 select_convert_fusion.4
  121.8 0.7 fusion.118
  122.5 0.7 fusion.112
  123.3 0.3 copy-done.8
  123.6 0.3 fusion.113
  123.9 0.3 fusion.119
  124.2 0.5 copy-done.9
  124.7 0.7 select_convert_fusion.5
  125.4 0.7 fusion.116
  126.2 0.7 fusion.114
  126.9 0.3 copy-done.5
  127.8 0.8 select_convert_fusion.4
  128.6 0.7 fusion.118
  129.3 0.7 fusion.112
  130.0 0.3 copy-done.8
  130.7 0.3 fusion.119
  131.0 0.5 copy-done.9
  131.4 1.6 copy.54
  133.0 1.1 all_to_all.116
  134.2 5.2 %all-to-all-start.4 = ((bf16[4,256,256]{2,1,0:T(8,128)(2,1)}), bf16[4,256,256]{2,1,0:T(8,128)(2,1)S(1)}, u32[]{:S(2)}, u32[]{:S(2)}) async-start(bf16[4,256,256]{2,1,0:T(8,128)(2,1)} %all_to_all.116), calls=%async_computation.4 | async-start | bytes 1048576 | tf_op jit(solution)/shard_map/all_to_all | solution.py:75
  139.4 0.5 copy.60
  139.9 1.1 all_to_all.128
  141.1 6.3 %all-to-all-done.4 = bf16[4,256,256]{2,1,0:T(8,128)(2,1)S(1)} async-done(((bf16[4,256,256]{2,1,0:T(8,128)(2,1)}), bf16[4,256,256]{2,1,0:T(8,128)(2,1)S(1)}, u32[]{:S(2)}, u32[]{:S(2)}) %all-to-all-start.4) | async-done | bytes 524320 | tf_op jit(solution)/shard_map/all_to_all | solution.py:75
  147.4 4.3 %all-to-all-start.7 = ((bf16[4,256,256]{2,1,0:T(8,128)(2,1)}), bf16[4,256,256]{2,1,0:T(8,128)(2,1)S(1)}, u32[]{:S(2)}, u32[]{:S(2)}) async-start(bf16[4,256,256]{2,1,0:T(8,128)(2,1)} %all_to_all.128), calls=%async_computation.7 | async-start | bytes 1048576 | tf_op jit(solution)/shard_map/all_to_all | solution.py:78
  151.7 0.5 copy.56
  152.2 1.1 all_to_all.120
  153.4 6.3 %all-to-all-done.7 = bf16[4,256,256]{2,1,0:T(8,128)(2,1)S(1)} async-done(((bf16[4,256,256]{2,1,0:T(8,128)(2,1)}), bf16[4,256,256]{2,1,0:T(8,128)(2,1)S(1)}, u32[]{:S(2)}, u32[]{:S(2)}) %all-to-all-start.7) | async-done | bytes 524320 | tf_op jit(solution)/shard_map/all_to_all | solution.py:78
  159.7 4.3 %all-to-all-start.5 = ((bf16[4,256,256]{2,1,0:T(8,128)(2,1)}), bf16[4,256,256]{2,1,0:T(8,128)(2,1)S(1)}, u32[]{:S(2)}, u32[]{:S(2)}) async-start(bf16[4,256,256]{2,1,0:T(8,128)(2,1)} %all_to_all.120), calls=%async_computation.5 | async-start | bytes 1048576 | tf_op jit(solution)/shard_map/all_to_all | solution.py:76
  164.0 0.5 copy.58
  164.5 1.1 all_to_all.124
  165.7 6.3 %all-to-all-done.5 = bf16[4,256,256]{2,1,0:T(8,128)(2,1)S(1)} async-done(((bf16[4,256,256]{2,1,0:T(8,128)(2,1)}), bf16[4,256,256]{2,1,0:T(8,128)(2,1)S(1)}, u32[]{:S(2)}, u32[]{:S(2)}) %all-to-all-start.5) | async-done | bytes 524320 | tf_op jit(solution)/shard_map/all_to_all | solution.py:76
  172.0 4.3 %all-to-all-start.6 = ((bf16[4,256,256]{2,1,0:T(8,128)(2,1)}), bf16[4,256,256]{2,1,0:T(8,128)(2,1)S(1)}, u32[]{:S(2)}, u32[]{:S(2)}) async-start(bf16[4,256,256]{2,1,0:T(8,128)(2,1)} %all_to_all.124), calls=%async_computation.6 | async-start | bytes 1048576 | tf_op jit(solution)/shard_map/all_to_all | solution.py:77
  176.5 1.0 copy.62
  177.7 1.0 copy.65
  178.9 1.0 copy.63
  179.9 4.4 %all-to-all-done.6 = bf16[4,256,256]{2,1,0:T(8,128)(2,1)S(1)} async-done(((bf16[4,256,256]{2,1,0:T(8,128)(2,1)}), bf16[4,256,256]{2,1,0:T(8,128)(2,1)S(1)}, u32[]{:S(2)}, u32[]{:S(2)}) %all-to-all-start.6) | async-done | bytes 524320 | tf_op jit(solution)/shard_map/all_to_all | solution.py:77
  184.5 1.0 copy.64
  (43 shorter events, 2.7 us)
Async XLA Ops:
  7.2 6.4 %copy-start = (bf16[256,1024]{1,0:T(8,128)(2,1)S(1)}, bf16[256,1024]{1,0:T(8,128)(2,1)}, u32[]{:S(2)}) copy-start(bf16[256,1024]{1,0:T(8,128)(2,1)} %param.8) | copy-start | bytes 1572868
  9.3 12.1 %all-to-all-start.1 = ((bf16[256,4,256]{0,2,1:T(8,128)(2,1)}), bf16[256,4,256]{0,2,1:T(8,128)(2,1)S(1)}, u32[]{:S(2)}, u32[]{:S(2)}) async-start(bf16[256,4,256]{0,2,1:T(8,128)(2,1)} %bitcast.13), calls=%async_computation.1 | async-start | bytes 1048576 | tf_op jit(solution)/shard_map/all_to_all | solution.py:53
  21.4 12.5 %all-to-all-start.2 = ((bf16[256,4,256]{2,0,1:T(8,128)(2,1)}), bf16[256,4,256]{2,0,1:T(8,128)(2,1)S(1)}, u32[]{:S(2)}, u32[]{:S(2)}) async-start(bf16[256,4,256]{2,0,1:T(8,128)(2,1)} %bitcast.105), calls=%async_computation.2 | async-start | bytes 1048576 | tf_op jit(solution)/shard_map/all_to_all | solution.py:54
  25.9 49.6 %all-gather.5.cloned.1.call-start = ((), (), s32[]{:S(2)}) async-start(), calls=%async_computation.8 | async-start | bytes 1179648 | tf_op jit(solution)/shard_map/all_gather | solution.py:64
  25.9 9.1 %copy-start.1 = (bf16[256,1024]{1,0:T(8,128)(2,1)S(1)}, bf16[256,1024]{1,0:T(8,128)(2,1)}, u32[]{:S(2)}) copy-start(bf16[256,1024]{1,0:T(8,128)(2,1)} %param.6) | copy-start | bytes 1572868
  33.8 6.4 %copy-start.2 = (bf16[256,1024]{1,0:T(8,128)(2,1)S(1)}, bf16[256,1024]{1,0:T(8,128)(2,1)}, u32[]{:S(2)}) copy-start(bf16[256,1024]{1,0:T(8,128)(2,1)} %param.9) | copy-start | bytes 1572868
  35.9 12.4 %all-to-all-start = ((bf16[256,4,256]{0,2,1:T(8,128)(2,1)}), bf16[256,4,256]{0,2,1:T(8,128)(2,1)S(1)}, u32[]{:S(2)}, u32[]{:S(2)}) async-start(bf16[256,4,256]{0,2,1:T(8,128)(2,1)} %bitcast.10), calls=%async_computation | async-start | bytes 1048576 | tf_op jit(solution)/shard_map/all_to_all | solution.py:52
  48.3 12.2 %all-to-all-start.3 = ((bf16[256,4,256]{2,0,1:T(8,128)(2,1)}), bf16[256,4,256]{2,0,1:T(8,128)(2,1)S(1)}, u32[]{:S(2)}, u32[]{:S(2)}) async-start(bf16[256,4,256]{2,0,1:T(8,128)(2,1)} %bitcast.104), calls=%async_computation.3 | async-start | bytes 1048576 | tf_op jit(solution)/shard_map/all_to_all | solution.py:55
  52.5 63.9 %all-gather.7.cloned.1.call-start = ((), (), s32[]{:S(2)}) async-start(), calls=%async_computation.9 | async-start | bytes 1179648 | tf_op jit(solution)/shard_map/all_gather | solution.py:65
  61.8 56.0 %copy-start.3 = (bf16[2,1024,128]{2,1,0:T(8,128)(2,1)S(1)}, bf16[2,1024,128]{2,1,0:T(8,128)(2,1)}, u32[]{:S(2)}) copy-start(bf16[2,1024,128]{2,1,0:T(8,128)(2,1)} %custom-call.3) | copy-start | bytes 1572868
  61.9 56.0 %copy-start.4 = (bf16[2,1024,128]{2,1,0:T(8,128)(2,1)S(1)}, bf16[2,1024,128]{2,1,0:T(8,128)(2,1)}, u32[]{:S(2)}) copy-start(bf16[2,1024,128]{2,1,0:T(8,128)(2,1)} %custom-call.2) | copy-start | bytes 1572868
  119.4 1.0 copy-start.5
  120.7 1.1 copy-start.6
  122.5 1.0 copy-start.8
  123.9 0.8 copy-start.9
  126.2 1.0 copy-start.5
  127.5 1.1 copy-start.6
  129.3 1.0 copy-start.8
  130.6 0.8 copy-start.9
  134.1 17.5 %copy-start.7 = (bf16[2,1024,128]{2,1,0:T(8,128)(2,1)S(1)}, bf16[2,1024,128]{2,1,0:T(8,128)(2,1)}, u32[]{:S(2)}) copy-start(bf16[2,1024,128]{2,1,0:T(8,128)(2,1)} %get-tuple-element.65) | copy-start | bytes 1572868
  134.2 13.2 %all-to-all-start.4 = ((bf16[4,256,256]{2,1,0:T(8,128)(2,1)}), bf16[4,256,256]{2,1,0:T(8,128)(2,1)S(1)}, u32[]{:S(2)}, u32[]{:S(2)}) async-start(bf16[4,256,256]{2,1,0:T(8,128)(2,1)} %all_to_all.116), calls=%async_computation.4 | async-start | bytes 1048576 | tf_op jit(solution)/shard_map/all_to_all | solution.py:75
  147.4 12.3 %all-to-all-start.7 = ((bf16[4,256,256]{2,1,0:T(8,128)(2,1)}), bf16[4,256,256]{2,1,0:T(8,128)(2,1)S(1)}, u32[]{:S(2)}, u32[]{:S(2)}) async-start(bf16[4,256,256]{2,1,0:T(8,128)(2,1)} %all_to_all.128), calls=%async_computation.7 | async-start | bytes 1048576 | tf_op jit(solution)/shard_map/all_to_all | solution.py:78
  159.7 12.3 %all-to-all-start.5 = ((bf16[4,256,256]{2,1,0:T(8,128)(2,1)}), bf16[4,256,256]{2,1,0:T(8,128)(2,1)S(1)}, u32[]{:S(2)}, u32[]{:S(2)}) async-start(bf16[4,256,256]{2,1,0:T(8,128)(2,1)} %all_to_all.120), calls=%async_computation.5 | async-start | bytes 1048576 | tf_op jit(solution)/shard_map/all_to_all | solution.py:76
  172.0 12.3 %all-to-all-start.6 = ((bf16[4,256,256]{2,1,0:T(8,128)(2,1)}), bf16[4,256,256]{2,1,0:T(8,128)(2,1)S(1)}, u32[]{:S(2)}, u32[]{:S(2)}) async-start(bf16[4,256,256]{2,1,0:T(8,128)(2,1)} %all_to_all.124), calls=%async_computation.6 | async-start | bytes 1048576 | tf_op jit(solution)/shard_map/all_to_all | solution.py:77
Sparse Core Ops, SparseCore 0:
  35.0 40.3 all-gather.4
  77.6 38.8 all-gather.6
where the time goes:
time: 194 us; the launch traced here: 192 us
  waiting for transfers between devices  105 us (54%)
  starting transfers between devices  35.5 us (18%)
  local copies, waits for them, and re-layouts  21.5 us (11%)
  between operations  14.2 us (7%)
  matrix products  13 us (7%)
  other arithmetic  2.74 us (1%)
    all_gather x1, waiting for transfers between devices, per_device(): qgrad_piece = lax.all_gather(qgrad[None], 'seq', axis=0, tiled=True)  39.7 us
    all_gather x1, waiting for transfers between devices, per_device(): state_piece = lax.all_gather(state[None], 'seq', axis=0, tiled=True)  13.6 us
    all_to_all x1, waiting for transfers between devices, per_device(): lax.all_to_all(query_rows, 'head', split_axis=1, concat_axis=0, tiled=True)  7.25 us
    all_to_all x1, waiting for transfers between devices, per_device(): lax.all_to_all(grad_rows, 'head', split_axis=1, concat_axis=0, tiled=True)  7.2 us
    all_to_all x1, waiting for transfers between devices, per_device(): lax.all_to_all(value_rows, 'head', split_axis=1, concat_axis=0, tiled=True)  7.19 us
    unnamed x18, local copies, waits for them, and re-layouts  7.14 us
    all_to_all x1, waiting for transfers between devices, per_device(): lax.all_to_all(key_rows, 'head', split_axis=1, concat_axis=0, tiled=True)  6.96 us
    all_to_all x1, waiting for transfers between devices, per_device(): lax.all_to_all(join_heads(attended), 'head', split_axis=0, concat_axis=1,...  6.31 us
  transfers between devices with their start and end apart: 10, of which 10 were waited for; matrix products, arithmetic and copies ran while one was open for 6% of the time, Pallas kernels for 0%

commit v1 on v0

v1 whole, which is shorter than its diff:
```python
import functools

import jax
import jax.numpy as jnp
from jax import lax
from jax.experimental import pallas as pl
from jax.experimental.pallas import tpu as pltpu
from jax.sharding import PartitionSpec as P

HEAD_DIM = 128
MESH = pl.DeviceIdType.MESH


def dot(a, b, ca, cb):
    return lax.dot_general(a, b, (((ca,), (cb,)), ((), ())), preferred_element_type=jnp.float32)


def kernel(nh, ns, nx, q_ref, k_ref, v_ref, g_ref, o_ref, gq_ref, gk_ref, gv_ref,
           part, got, zpart, zgot, back, pre, acc,
           send1, recv1, send3, recv3, send4, recv4):
    tokens, width = q_ref.shape
    heads = width // HEAD_DIM
    group = nh * nx
    planes = ns // nx
    rows = width // group
    head_at, seq_at = lax.axis_index("head"), lax.axis_index("seq")
    z, me = seq_at // nx, lax.rem(seq_at, nx) * nh + head_at

    def in_plane(p):
        return {"head": lax.rem(p, nh), "seq": z * nx + p // nh}

    def in_column(zz):
        return {"head": head_at, "seq": zz * nx + lax.rem(seq_at, nx)}

    def rows_of(p):
        start = p * rows
        return pl.ds(start if isinstance(start, int) else pl.multiple_of(start, rows), rows)

    barrier = pltpu.get_barrier_semaphore()
    for k in range(1, group):
        pl.semaphore_signal(barrier, inc=1, device_id=in_plane(lax.rem(me + k, group)), device_id_type=MESH)
    for k in range(1, planes):
        pl.semaphore_signal(barrier, inc=1, device_id=in_column(lax.rem(z + k, planes)), device_id_type=MESH)

    for h in range(heads):
        cols = slice(h * HEAD_DIM, (h + 1) * HEAD_DIM)
        part[0, cols, :] = dot(k_ref[:, cols], v_ref[:, cols], 0, 0).astype(part.dtype)
        part[1, cols, :] = dot(q_ref[:, cols], g_ref[:, cols], 0, 0).astype(part.dtype)

    pl.semaphore_wait(barrier, group + planes - 2)

    def copy1(dst_p, slot):
        return pltpu.make_async_remote_copy(
            src_ref=part.at[:, rows_of(dst_p), :], dst_ref=got.at[slot],
            send_sem=send1.at[dst_p], recv_sem=recv1.at[slot],
            device_id=in_plane(dst_p), device_id_type=MESH)

    for k in range(1, group):
        copy1(lax.rem(me + k, group), me).start()
    got[me] = part[:, rows_of(me), :]

    causal = (lax.broadcasted_iota(jnp.int32, (tokens, tokens), 1)
              <= lax.broadcasted_iota(jnp.int32, (tokens, tokens), 0))
    for h in range(heads):
        cols = slice(h * HEAD_DIM, (h + 1) * HEAD_DIM)
        q, kk, v, g = q_ref[:, cols], k_ref[:, cols], v_ref[:, cols], g_ref[:, cols]
        scores = jnp.where(causal, dot(q, kk, 1, 1), 0.0).astype(jnp.bfloat16)
        dprob = jnp.where(causal, dot(g, v, 1, 1), 0.0).astype(jnp.bfloat16)
        acc[0, :, cols] = dot(scores, v, 1, 0)
        acc[1, :, cols] = dot(dprob, kk, 1, 0)
        acc[2, :, cols] = dot(dprob, q, 0, 0)
        acc[3, :, cols] = dot(scores, g, 0, 0)

    for k in range(1, group):
        source = lax.rem(me + group - k, group)
        copy1(source, source).wait_recv()

    total = got[0].astype(jnp.float32)
    for p in range(1, group):
        total = total + got[p].astype(jnp.float32)
    zpart[...] = total.astype(zpart.dtype)

    def copy3(which, zz, slot):
        return pltpu.make_async_remote_copy(
            src_ref=zpart.at[which], dst_ref=zgot.at[which, slot],
            send_sem=send3.at[which, zz], recv_sem=recv3.at[which, slot],
            device_id=in_column(zz), device_id_type=MESH)

    for zz in range(planes):
        @pl.when(zz > z)
        def _():
            copy3(0, zz, z).start()

        @pl.when(zz < z)
        def _():
            copy3(1, zz, z).start()

    for zz in range(planes):
        @pl.when(zz >= z)
        def _():
            zgot[0, zz] = jnp.zeros(zgot.shape[2:], zgot.dtype)

        @pl.when(zz <= z)
        def _():
            zgot[1, zz] = jnp.zeros(zgot.shape[2:], zgot.dtype)

    for zz in range(planes):
        @pl.when(zz < z)
        def _():
            copy3(0, zz, zz).wait_recv()

        @pl.when(zz > z)
        def _():
            copy3(1, zz, zz).wait_recv()

    run = zgot[0, 0].astype(jnp.float32)
    for zz in range(1, planes):
        run = run + zgot[0, zz].astype(jnp.float32)
    for p in range(group):
        back[p, 0] = run.astype(jnp.bfloat16)
        if p < group - 1:
            run = run + got[p, 0].astype(jnp.float32)
    run = zgot[1, 0].astype(jnp.float32)
    for zz in range(1, planes):
        run = run + zgot[1, zz].astype(jnp.float32)
    for p in range(group - 1, -1, -1):
        back[p, 1] = run.astype(jnp.bfloat16)
        if p > 0:
            run = run + got[p, 1].astype(jnp.float32)

    def copy4(dst_p, owner):
        return pltpu.make_async_remote_copy(
            src_ref=back.at[dst_p], dst_ref=pre.at[:, rows_of(owner), :],
            send_sem=send4.at[dst_p], recv_sem=recv4.at[owner],
            device_id=in_plane(dst_p), device_id_type=MESH)

    for k in range(1, group):
        copy4(lax.rem(me + k, group), me).start()
    pre[:, rows_of(me), :] = back[me]
    for k in range(1, group):
        source = lax.rem(me + group - k, group)
        copy4(source, source).wait_recv()

    for h in range(heads):
        cols = slice(h * HEAD_DIM, (h + 1) * HEAD_DIM)
        q, kk, v, g = q_ref[:, cols], k_ref[:, cols], v_ref[:, cols], g_ref[:, cols]
        prefix, suffix = pre[0, cols, :], pre[1, cols, :]
        o_ref[:, cols] = (acc[0, :, cols] + dot(q, prefix, 1, 0)).astype(jnp.bfloat16)
        gq_ref[:, cols] = (acc[1, :, cols] + dot(g, prefix, 1, 1)).astype(jnp.bfloat16)
        gk_ref[:, cols] = (acc[2, :, cols] + dot(v, suffix, 1, 1)).astype(jnp.bfloat16)
        gv_ref[:, cols] = (acc[3, :, cols] + dot(kk, suffix, 1, 0)).astype(jnp.bfloat16)

    for k in range(1, group):
        there = lax.rem(me + k, group)
        copy1(there, me).wait_send()
        copy4(there, me).wait_send()
    for zz in range(planes):
        @pl.when(zz > z)
        def _():
            copy3(0, zz, z).wait_send()

        @pl.when(zz < z)
        def _():
            copy3(1, zz, z).wait_send()


def per_device(nh, ns, query_rows, key_rows, value_rows, grad_rows):
    tokens, width = query_rows.shape
    nx = 1
    while 2 * (2 * nx) ** 2 <= ns and ns % (2 * nx) == 0:
        nx *= 2
    group, planes = nh * nx, ns // nx
    rows = width // group
    bf16, f32 = jnp.bfloat16, jnp.float32
    vmem = pl.BlockSpec(memory_space=pltpu.VMEM)
    return pl.pallas_call(
        functools.partial(kernel, nh, ns, nx),
        out_shape=(jax.ShapeDtypeStruct((tokens, width), bf16),) * 4,
        in_specs=[vmem] * 4,
        out_specs=(vmem,) * 4,
        scratch_shapes=[
            pltpu.VMEM((2, width, HEAD_DIM), bf16),
            pltpu.VMEM((group, 2, rows, HEAD_DIM), bf16),
            pltpu.VMEM((2, rows, HEAD_DIM), bf16),
            pltpu.VMEM((2, planes, rows, HEAD_DIM), bf16),
            pltpu.VMEM((group, 2, rows, HEAD_DIM), bf16),
            pltpu.VMEM((2, width, HEAD_DIM), bf16),
            pltpu.VMEM((4, tokens, width), f32),
            pltpu.SemaphoreType.DMA((group,)),
            pltpu.SemaphoreType.DMA((group,)),
            pltpu.SemaphoreType.DMA((2, planes)),
            pltpu.SemaphoreType.DMA((2, planes)),
            pltpu.SemaphoreType.DMA((group,)),
            pltpu.SemaphoreType.DMA((group,)),
        ],
        compiler_params=pltpu.CompilerParams(
            collective_id=0, has_side_effects=True, vmem_limit_bytes=48 * 1024 * 1024),
        cost_estimate=pl.CostEstimate(
            flops=tokens * width * (8 * tokens + 12 * HEAD_DIM),
            bytes_accessed=16 * tokens * width, transcendentals=0),
    )(query_rows, key_rows, value_rows, grad_rows)


def solution(mesh):
    placed = P(("seq", "head"), None)
    return jax.shard_map(
        functools.partial(per_device, mesh.shape["head"], mesh.shape["seq"]),
        mesh=mesh,
        in_specs=(placed,) * 4,
        out_specs=(placed,) * 4,
        check_vma=False,
    )
```

time: 194 us -> 33.2 us (0.17)
  waiting for transfers between devices: 105 us -> 0 us
  starting transfers between devices: 35.5 us -> 0 us
  Pallas kernels: 0 us -> 24.9 us
  local copies, waits for them, and re-layouts: 21.5 us -> 7.33 us
  between operations: 14.2 us -> 0.65 us
  matrix products: 13 us -> 0 us
  other arithmetic: 2.74 us -> 0 us
    all_gather x2 -> x0, waiting for transfers between devices: 53.3 us -> none  [the longest x1 39.7 us: per_device(): qgrad_piece = lax.all_gather(qgrad[None], 'seq', axis=0, tiled=True)]
    all_to_all x8 -> x0, waiting for transfers between devices: 51.9 us -> none  [the longest x1 7.25 us: per_device(): lax.all_to_all(query_rows, 'head', split_axis=1, concat_axis=0, tiled=True)]
    all_to_all x8 -> x0, starting transfers between devices: 35.5 us -> none  [the longest x1 5.25 us: per_device(): lax.all_to_all(join_heads(attended), 'head', split_axis=0, concat_axis=1,...]
    pallas_call x0 -> x1, Pallas kernels: none -> 24.9 us  [per_device(): pl.pallas_call(functools.partial(kernel, nh, ns, nx), out_shape=(jax.Shap...]
    dot_general x22 -> x0, matrix products: 13 us -> none  [the longest x2 1.54 us: one_head(): jnp.einsum('td,sd->ts', query, keyset, preferred_element_type=jnp.float32)]
    all_to_all x12 -> x0, local copies, waits for them, and re-layouts: 7.78 us -> none  [the longest x2 1.33 us: per_device(): lax.all_to_all(join_heads(grad_key), 'head', split_axis=0, concat_axis=1,...]
    transpose x5 -> x0, local copies, waits for them, and re-layouts: 3.34 us -> none  [the longest x4 3.2 us: join_heads(): jnp.transpose(blocks, (1, 0, 2))]
    reduce_sum x2 -> x0, other arithmetic: 2.73 us -> none  [the longest x1 1.36 us: per_device(): prefix = jnp.sum(state_piece * before, axis=0)]
  transfers between devices with their start and end apart: 10 -> 0, of which waited for: 10 -> 0; matrix products, arithmetic and copies ran while one was open for 6% -> 0% of each run, Pallas kernels for 0% -> 0%
where the time goes in v1:
time: 33.2 us; the launch traced here: 32.8 us
  Pallas kernels  24.9 us (75%)
  local copies, waits for them, and re-layouts  7.33 us (22%)
  between operations  0.65 us (2%)
    pallas_call x1, Pallas kernels, per_device(): pl.pallas_call(functools.partial(kernel, nh, ns, nx), out_shape=(jax.Shap...  24.9 us
    unnamed x12, local copies, waits for them, and re-layouts  7.33 us

profile of v1, /device:TPU:1, one launch (start us, length us, event | category | flops | bytes accessed | tf_op | source)
XLA Modules:
  0.0 32.8 jit_solution(7492479178875457689)
XLA Ops:
  0.6 0.0 copy-start
  0.6 1.0 %copy-done = bf16[256,1024]{1,0:T(8,128)(2,1)S(1)} copy-done((bf16[256,1024]{1,0:T(8,128)(2,1)S(1)}, bf16[256,1024]{1,0:T(8,128)(2,1)}, u32[]{:S(2)}) %copy-start) | copy-done | bytes 524312
  1.7 0.0 copy-start.1
  1.7 1.0 %copy-done.1 = bf16[256,1024]{1,0:T(8,128)(2,1)S(1)} copy-done((bf16[256,1024]{1,0:T(8,128)(2,1)S(1)}, bf16[256,1024]{1,0:T(8,128)(2,1)}, u32[]{:S(2)}) %copy-start.1) | copy-done | bytes 524312
  2.7 0.0 copy-start.2
  2.7 1.0 %copy-done.2 = bf16[256,1024]{1,0:T(8,128)(2,1)S(1)} copy-done((bf16[256,1024]{1,0:T(8,128)(2,1)S(1)}, bf16[256,1024]{1,0:T(8,128)(2,1)}, u32[]{:S(2)}) %copy-start.2) | copy-done | bytes 524312
  3.8 0.0 copy-start.3
  3.8 1.0 %copy-done.3 = bf16[256,1024]{1,0:T(8,128)(2,1)S(1)} copy-done((bf16[256,1024]{1,0:T(8,128)(2,1)S(1)}, bf16[256,1024]{1,0:T(8,128)(2,1)}, u32[]{:S(2)}) %copy-start.3) | copy-done | bytes 524312
  4.8 24.9 %shard_map.75 = (bf16[256,1024]{1,0:T(8,128)(2,1)S(1)}, bf16[256,1024]{1,0:T(8,128)(2,1)S(1)}, bf16[256,1024]{1,0:T(8,128)(2,1)S(1)}, bf16[256,1024]{1,0:T(8,128)(2,1)S(1)}) custom-call(bf16[256,1024]{1,0:T(8,128)(2,1)S(1)} %copy-done, bf16[256,1024]{1,0:T(8,128)(2,1)S(1)} %copy-done.1, bf16[256,1024]{1,0:T(8,128)(2,1)S(1)} %copy-done.2, ...), custom_call_target="tpu_custom_call" | custom-call | flops 939524096 | bytes 4194304 | tf_op jit(solution)/shard_map/pallas_call | solution.py:176
  29.7 0.8 %copy.12 = bf16[256,1024]{1,0:T(8,128)(2,1)} copy(bf16[256,1024]{1,0:T(8,128)(2,1)S(1)} %get-tuple-element.8) | data formatting | bytes 1048576
  30.5 0.8 %copy.13 = bf16[256,1024]{1,0:T(8,128)(2,1)} copy(bf16[256,1024]{1,0:T(8,128)(2,1)S(1)} %get-tuple-element.9) | data formatting | bytes 1048576
  31.3 0.8 %copy.14 = bf16[256,1024]{1,0:T(8,128)(2,1)} copy(bf16[256,1024]{1,0:T(8,128)(2,1)S(1)} %get-tuple-element.10) | data formatting | bytes 1048576
  32.1 0.8 %copy.15 = bf16[256,1024]{1,0:T(8,128)(2,1)} copy(bf16[256,1024]{1,0:T(8,128)(2,1)S(1)} %get-tuple-element.11) | data formatting | bytes 1048576
Async XLA Ops:
  0.6 1.0 %copy-start = (bf16[256,1024]{1,0:T(8,128)(2,1)S(1)}, bf16[256,1024]{1,0:T(8,128)(2,1)}, u32[]{:S(2)}) copy-start(bf16[256,1024]{1,0:T(8,128)(2,1)} %q_ref.1) | copy-start | bytes 1572868
  1.7 1.0 %copy-start.1 = (bf16[256,1024]{1,0:T(8,128)(2,1)S(1)}, bf16[256,1024]{1,0:T(8,128)(2,1)}, u32[]{:S(2)}) copy-start(bf16[256,1024]{1,0:T(8,128)(2,1)} %k_ref.1) | copy-start | bytes 1572868
  2.7 1.0 %copy-start.2 = (bf16[256,1024]{1,0:T(8,128)(2,1)S(1)}, bf16[256,1024]{1,0:T(8,128)(2,1)}, u32[]{:S(2)}) copy-start(bf16[256,1024]{1,0:T(8,128)(2,1)} %v_ref.1) | copy-start | bytes 1572868
  3.8 1.0 %copy-start.3 = (bf16[256,1024]{1,0:T(8,128)(2,1)S(1)}, bf16[256,1024]{1,0:T(8,128)(2,1)}, u32[]{:S(2)}) copy-start(bf16[256,1024]{1,0:T(8,128)(2,1)} %g_ref.1) | copy-start | bytes 1572868

commit v2 on v0

v2 whole, which is shorter than its diff:
```python
import functools

import jax
import jax.numpy as jnp
from jax import lax
from jax.experimental import pallas as pl
from jax.experimental.pallas import tpu as pltpu
from jax.sharding import PartitionSpec as P

HEAD_DIM = 128
CORES = 2
MESH = pl.DeviceIdType.MESH


def dot(a, b, ca, cb):
    return lax.dot_general(a, b, (((ca,), (cb,)), ((), ())), preferred_element_type=jnp.float32)


def states_kernel(nh, ns, nx, q_hbm, k_hbm, v_hbm, g_hbm, o_ref, gq_ref, gk_ref, gv_ref,
                  q_ref, k_ref, v_ref, g_ref, other, paired, own, chip, got, zpart, zgot,
                  back, chippre, mate, pre, acc,
                  in_sem, send0, recv0, send1, recv1, send2, recv2, send3, recv3, send4, recv4):
    tokens, width = q_ref.shape
    heads = width // HEAD_DIM
    half = heads // CORES
    along = nh // CORES
    chips = along * nx
    planes = ns // nx
    half_rows = half * HEAD_DIM
    rows = half_rows // chips
    head_at, seq_at = lax.axis_index("head"), lax.axis_index("seq")
    core = lax.rem(head_at, CORES)
    z = seq_at // nx
    me = lax.rem(seq_at, nx) * along + head_at // CORES
    first, mine = core * half, (1 - core) * half
    partner = {"head": head_at + 1 - 2 * core, "seq": seq_at}

    def in_plane(p):
        return {"head": lax.rem(p, along) * CORES + core, "seq": z * nx + p // along}

    def in_column(zz):
        return {"head": head_at, "seq": zz * nx + lax.rem(seq_at, nx)}

    def rows_of(p):
        return pl.ds(pl.multiple_of(p * rows, rows), rows)

    def cols_of(h):
        return pl.ds(pl.multiple_of(h * HEAD_DIM, HEAD_DIM), HEAD_DIM)

    loads = [pltpu.make_async_copy(src, dst, in_sem.at[i]) for i, (src, dst) in enumerate(
        ((k_hbm, k_ref), (v_hbm, v_ref), (q_hbm, q_ref), (g_hbm, g_ref)))]
    for load in loads:
        load.start()

    barrier = pltpu.get_barrier_semaphore()
    pl.semaphore_signal(barrier, inc=1, device_id=partner, device_id_type=MESH)
    for k in range(1, chips):
        pl.semaphore_signal(barrier, inc=1, device_id=in_plane(lax.rem(me + k, chips)), device_id_type=MESH)
    for k in range(1, planes):
        pl.semaphore_signal(barrier, inc=1, device_id=in_column(lax.rem(z + k, planes)), device_id_type=MESH)

    def copy0(a):
        return pltpu.make_async_remote_copy(
            src_ref=other.at[a], dst_ref=paired.at[a], send_sem=send0.at[a], recv_sem=recv0.at[a],
            device_id=partner, device_id_type=MESH)

    def copy1(a, there, slot):
        return pltpu.make_async_remote_copy(
            src_ref=chip.at[a, rows_of(there), :], dst_ref=got.at[slot, a],
            send_sem=send1.at[a, there], recv_sem=recv1.at[a, slot],
            device_id=in_plane(there), device_id_type=MESH)

    def copy2(a, zz, slot):
        return pltpu.make_async_remote_copy(
            src_ref=zpart.at[a], dst_ref=zgot.at[a, slot],
            send_sem=send2.at[a, zz], recv_sem=recv2.at[a, slot],
            device_id=in_column(zz), device_id_type=MESH)

    def copy3(a, there, owner):
        return pltpu.make_async_remote_copy(
            src_ref=back.at[there, a], dst_ref=chippre.at[a, rows_of(owner), :],
            send_sem=send3.at[a, there], recv_sem=recv3.at[a, owner],
            device_id=in_plane(there), device_id_type=MESH)

    def copy4(a, whose):
        return pltpu.make_async_remote_copy(
            src_ref=mate.at[a],
            dst_ref=pre.at[a, pl.ds(pl.multiple_of(whose * half_rows, half_rows), half_rows), :],
            send_sem=send4.at[a], recv_sem=recv4.at[a], device_id=partner, device_id_type=MESH)

    for a, (x_ref, y_ref) in enumerate(((k_ref, v_ref), (q_ref, g_ref))):
        loads[2 * a].wait()
        loads[2 * a + 1].wait()
        for h in range(half):
            cols, at = cols_of(mine + h), slice(h * HEAD_DIM, (h + 1) * HEAD_DIM)
            other[a, at, :] = dot(x_ref[:, cols], y_ref[:, cols], 0, 0).astype(other.dtype)
        if a == 0:
            pl.semaphore_wait(barrier, chips + planes - 1)
        copy0(a).start()
        for h in range(half):
            cols, at = cols_of(first + h), slice(h * HEAD_DIM, (h + 1) * HEAD_DIM)
            own[a, at, :] = dot(x_ref[:, cols], y_ref[:, cols], 0, 0)

    for a in range(2):
        copy0(a).wait_recv()
        chip[a] = (own[a] + paired[a].astype(jnp.float32)).astype(chip.dtype)
        for k in range(1, chips):
            copy1(a, lax.rem(me + k, chips), me).start()
        got[me, a] = chip[a, rows_of(me), :]

    causal = (lax.broadcasted_iota(jnp.int32, (tokens, tokens), 1)
              <= lax.broadcasted_iota(jnp.int32, (tokens, tokens), 0))

    def within(begin, end):
        for h in range(begin, end):
            cols = slice(h * HEAD_DIM, (h + 1) * HEAD_DIM)
            q, kk, v, g = q_ref[:, cols], k_ref[:, cols], v_ref[:, cols], g_ref[:, cols]
            scores = jnp.where(causal, dot(q, kk, 1, 1), 0.0).astype(jnp.bfloat16)
            dprob = jnp.where(causal, dot(g, v, 1, 1), 0.0).astype(jnp.bfloat16)
            acc[0, :, cols] = dot(scores, v, 1, 0)
            acc[1, :, cols] = dot(dprob, kk, 1, 0)
            acc[2, :, cols] = dot(dprob, q, 0, 0)
            acc[3, :, cols] = dot(scores, g, 0, 0)

    cut1, cut2 = heads * 3 // 8, heads * 5 // 8
    within(0, cut1)

    for a in range(2):
        for k in range(1, chips):
            source = lax.rem(me + chips - k, chips)
            copy1(a, source, source).wait_recv()
        total = got[0, a].astype(jnp.float32)
        for p in range(1, chips):
            total = total + got[p, a].astype(jnp.float32)
        zpart[a] = total.astype(zpart.dtype)
        for zz in range(planes):
            @pl.when(zz > z if a == 0 else zz < z)
            def _():
                copy2(a, zz, z).start()

    for a in range(2):
        for zz in range(planes):
            @pl.when(zz >= z if a == 0 else zz <= z)
            def _():
                zgot[a, zz] = jnp.zeros(zgot.shape[2:], zgot.dtype)

    within(cut1, cut2)

    for a in range(2):
        for zz in range(planes):
            @pl.when(zz < z if a == 0 else zz > z)
            def _():
                copy2(a, zz, zz).wait_recv()
        run = zgot[a, 0].astype(jnp.float32)
        for zz in range(1, planes):
            run = run + zgot[a, zz].astype(jnp.float32)
        order = range(chips) if a == 0 else range(chips - 1, -1, -1)
        for p in order:
            back[p, a] = run.astype(jnp.bfloat16)
            run = run + got[p, a].astype(jnp.float32)
        for k in range(1, chips):
            copy3(a, lax.rem(me + k, chips), me).start()
        chippre[a, rows_of(me), :] = back[me, a]

    within(cut2, heads)

    my_rows = pl.ds(pl.multiple_of(core * half_rows, half_rows), half_rows)
    for a in range(2):
        for k in range(1, chips):
            source = lax.rem(me + chips - k, chips)
            copy3(a, source, source).wait_recv()
        base = chippre[a].astype(jnp.float32)
        later = core == (1 if a == 0 else 0)
        mate[a] = (base + jnp.where(later, 0.0, own[a])).astype(jnp.bfloat16)
        copy4(a, core).start()
        pre[a, my_rows, :] = (base + jnp.where(later, paired[a].astype(jnp.float32), 0.0)).astype(jnp.bfloat16)

    def finish(start):
        for h in range(half):
            cols = cols_of(start + h)
            q, kk, v, g = q_ref[:, cols], k_ref[:, cols], v_ref[:, cols], g_ref[:, cols]
            prefix, suffix = pre[0, cols, :], pre[1, cols, :]
            o_ref[:, cols] = (acc[0, :, cols] + dot(q, prefix, 1, 0)).astype(jnp.bfloat16)
            gq_ref[:, cols] = (acc[1, :, cols] + dot(g, prefix, 1, 1)).astype(jnp.bfloat16)
            gk_ref[:, cols] = (acc[2, :, cols] + dot(v, suffix, 1, 1)).astype(jnp.bfloat16)
            gv_ref[:, cols] = (acc[3, :, cols] + dot(kk, suffix, 1, 0)).astype(jnp.bfloat16)

    finish(first)
    for a in range(2):
        copy4(a, 1 - core).wait_recv()
    finish(mine)

    for a in range(2):
        copy0(a).wait_send()
        copy4(a, core).wait_send()
        for k in range(1, chips):
            there = lax.rem(me + k, chips)
            copy1(a, there, me).wait_send()
            copy3(a, there, me).wait_send()
        for zz in range(planes):
            @pl.when(zz > z if a == 0 else zz < z)
            def _():
                copy2(a, zz, z).wait_send()


def store_kernel(*refs):
    sources, targets, sem = refs[:4], refs[4:8], refs[8]
    copies = [pltpu.make_async_copy(s, t, sem.at[i]) for i, (s, t) in enumerate(zip(sources, targets))]
    for copy in copies:
        copy.start()
    for copy in copies:
        copy.wait()


def per_device(nh, ns, query_rows, key_rows, value_rows, grad_rows):
    tokens, width = query_rows.shape
    nx = 1
    while 2 * (2 * nx) ** 2 <= ns and ns % (2 * nx) == 0:
        nx *= 2
    chips, planes = nh // CORES * nx, ns // nx
    half_rows = width // CORES
    rows = half_rows // chips
    bf16, f32 = jnp.bfloat16, jnp.float32
    vmem, hbm = pl.BlockSpec(memory_space=pltpu.VMEM), pl.BlockSpec(memory_space=pltpu.HBM)
    dma = pltpu.SemaphoreType.DMA
    shape = (jax.ShapeDtypeStruct((tokens, width), bf16),) * 4
    results = pl.pallas_call(
        functools.partial(states_kernel, nh, ns, nx),
        out_shape=shape,
        in_specs=[hbm] * 4,
        out_specs=(vmem,) * 4,
        scratch_shapes=[pltpu.VMEM((tokens, width), bf16)] * 4 + [
            pltpu.VMEM((2, half_rows, HEAD_DIM), f32),
            pltpu.VMEM((2, half_rows, HEAD_DIM), f32),
            pltpu.VMEM((2, half_rows, HEAD_DIM), f32),
            pltpu.VMEM((2, half_rows, HEAD_DIM), bf16),
            pltpu.VMEM((chips, 2, rows, HEAD_DIM), bf16),
            pltpu.VMEM((2, rows, HEAD_DIM), bf16),
            pltpu.VMEM((2, planes, rows, HEAD_DIM), bf16),
            pltpu.VMEM((chips, 2, rows, HEAD_DIM), bf16),
            pltpu.VMEM((2, half_rows, HEAD_DIM), bf16),
            pltpu.VMEM((2, half_rows, HEAD_DIM), bf16),
            pltpu.VMEM((2, width, HEAD_DIM), bf16),
            pltpu.VMEM((4, tokens, width), f32),
            dma((4,)), dma((2,)), dma((2,)), dma((2, chips)), dma((2, chips)),
            dma((2, planes)), dma((2, planes)), dma((2, chips)), dma((2, chips)), dma((2,)), dma((2,)),
        ],
        compiler_params=pltpu.CompilerParams(
            collective_id=0, has_side_effects=True, vmem_limit_bytes=103 * 512 * 1024),
        cost_estimate=pl.CostEstimate(
            flops=tokens * width * (8 * tokens + 12 * HEAD_DIM),
            bytes_accessed=16 * tokens * width, transcendentals=0),
    )(query_rows, key_rows, value_rows, grad_rows)
    return pl.pallas_call(
        store_kernel,
        out_shape=shape,
        in_specs=[vmem] * 4,
        out_specs=(hbm,) * 4,
        scratch_shapes=[dma((4,))],
        compiler_params=pltpu.CompilerParams(vmem_limit_bytes=8 * 1024 * 1024),
        cost_estimate=pl.CostEstimate(flops=0, bytes_accessed=16 * tokens * width, transcendentals=0),
    )(*results)


def solution(mesh):
    placed = P(("seq", "head"), None)
    return jax.shard_map(
        functools.partial(per_device, mesh.shape["head"], mesh.shape["seq"]),
        mesh=mesh,
        in_specs=(placed,) * 4,
        out_specs=(placed,) * 4,
        check_vma=False,
    )
```

time: 194 us -> 24 us (0.12)
  waiting for transfers between devices: 105 us -> 0 us
  starting transfers between devices: 35.5 us -> 0 us
  Pallas kernels: 0 us -> 23.2 us
  local copies, waits for them, and re-layouts: 21.5 us -> 0 us
  between operations: 14.2 us -> 0.64 us
  matrix products: 13 us -> 0 us
  other arithmetic: 2.74 us -> 0 us
    all_gather x2 -> x0, waiting for transfers between devices: 53.3 us -> none  [the longest x1 39.7 us: per_device(): qgrad_piece = lax.all_gather(qgrad[None], 'seq', axis=0, tiled=True)]
    all_to_all x8 -> x0, waiting for transfers between devices: 51.9 us -> none  [the longest x1 7.25 us: per_device(): lax.all_to_all(query_rows, 'head', split_axis=1, concat_axis=0, tiled=True)]
    all_to_all x8 -> x0, starting transfers between devices: 35.5 us -> none  [the longest x1 5.25 us: per_device(): lax.all_to_all(join_heads(attended), 'head', split_axis=0, concat_axis=1,...]
    pallas_call x0 -> x2, Pallas kernels: none -> 23.2 us  [the longest x1 21.9 us: per_device(): pl.pallas_call(functools.partial(states_kernel, nh, ns, nx), out_shape=sh...]
    dot_general x22 -> x0, matrix products: 13 us -> none  [the longest x2 1.54 us: one_head(): jnp.einsum('td,sd->ts', query, keyset, preferred_element_type=jnp.float32)]
    all_to_all x12 -> x0, local copies, waits for them, and re-layouts: 7.78 us -> none  [the longest x2 1.33 us: per_device(): lax.all_to_all(join_heads(grad_key), 'head', split_axis=0, concat_axis=1,...]
    unnamed x18 -> x0, local copies, waits for them, and re-layouts: 7.14 us -> none
    transpose x5 -> x0, local copies, waits for them, and re-layouts: 3.34 us -> none  [the longest x4 3.2 us: join_heads(): jnp.transpose(blocks, (1, 0, 2))]
  transfers between devices with their start and end apart: 10 -> 0, of which waited for: 10 -> 0; matrix products, arithmetic and copies ran while one was open for 6% -> 0% of each run, Pallas kernels for 0% -> 0%
where the time goes in v2:
time: 24 us; the launch traced here: 23.9 us
  Pallas kernels  23.2 us (97%)
  between operations  0.64 us (3%)
    pallas_call x1, Pallas kernels, per_device(): pl.pallas_call(functools.partial(states_kernel, nh, ns, nx), out_shape=sh...  21.9 us
    pallas_call x1, Pallas kernels, per_device(): pl.pallas_call(store_kernel, out_shape=shape, in_specs=[vmem] * 4, out_sp...  1.35 us

profile of v2, /device:TPU:1, one launch (start us, length us, event | category | flops | bytes accessed | tf_op | source)
XLA Modules:
  0.0 23.9 jit_solution(12278335277504926924)
XLA Ops:
  0.6 21.9 %shard_map.75 = (bf16[256,1024]{1,0:T(8,128)(2,1)S(1)}, bf16[256,1024]{1,0:T(8,128)(2,1)S(1)}, bf16[256,1024]{1,0:T(8,128)(2,1)S(1)}, bf16[256,1024]{1,0:T(8,128)(2,1)S(1)}) custom-call(bf16[256,1024]{1,0:T(8,128)(2,1)} %q_hbm.1, bf16[256,1024]{1,0:T(8,128)(2,1)} %k_hbm.1, bf16[256,1024]{1,0:T(8,128)(2,1)} %v_hbm.1, bf16[256,1024]{1,0:T(8,128)(2,1)} %g_hbm.1), custom_call_target="tpu_custom_call" | custom-call | flops 939524096 | bytes 4194304 | tf_op jit(solution)/shard_map/pallas_call | solution.py:227
  22.5 1.3 %shard_map.76 = (bf16[256,1024]{1,0:T(8,128)(2,1)}, bf16[256,1024]{1,0:T(8,128)(2,1)}, bf16[256,1024]{1,0:T(8,128)(2,1)}, bf16[256,1024]{1,0:T(8,128)(2,1)}) custom-call(bf16[256,1024]{1,0:T(8,128)(2,1)S(1)} %get-tuple-element.8.refs_0_, bf16[256,1024]{1,0:T(8,128)(2,1)S(1)} %get-tuple-element.9.refs_1_, bf16[256,1024]{1,0:T(8,128)(2,1)S(1)} %get-tuple-element.10.refs_2_, ...), custom_call_target="tpu_custom_call" | custom-call | bytes 4194304 | tf_op jit(solution)/shard_map/pallas_call | solution.py:254

commit v3 on v2

--- a/solution.py
+++ b/solution.py
@@ -88,25 +88,32 @@
             dst_ref=pre.at[a, pl.ds(pl.multiple_of(whose * half_rows, half_rows), half_rows), :],
             send_sem=send4.at[a], recv_sem=recv4.at[a], device_id=partner, device_id_type=MESH)
 
-    for a, (x_ref, y_ref) in enumerate(((k_ref, v_ref), (q_ref, g_ref))):
-        loads[2 * a].wait()
-        loads[2 * a + 1].wait()
+    def states_of(a, start, out):
+        x_ref, y_ref = ((k_ref, v_ref), (q_ref, g_ref))[a]
         for h in range(half):
-            cols, at = cols_of(mine + h), slice(h * HEAD_DIM, (h + 1) * HEAD_DIM)
-            other[a, at, :] = dot(x_ref[:, cols], y_ref[:, cols], 0, 0).astype(other.dtype)
-        if a == 0:
-            pl.semaphore_wait(barrier, chips + planes - 1)
-        copy0(a).start()
-        for h in range(half):
-            cols, at = cols_of(first + h), slice(h * HEAD_DIM, (h + 1) * HEAD_DIM)
-            own[a, at, :] = dot(x_ref[:, cols], y_ref[:, cols], 0, 0)
-
-    for a in range(2):
+            cols, at = cols_of(start + h), slice(h * HEAD_DIM, (h + 1) * HEAD_DIM)
+            out[a, at, :] = dot(x_ref[:, cols], y_ref[:, cols], 0, 0)
+
+    def chip_sums(a):
         copy0(a).wait_recv()
-        chip[a] = (own[a] + paired[a].astype(jnp.float32)).astype(chip.dtype)
+        chip[a] = (own[a] + paired[a]).astype(chip.dtype)
         for k in range(1, chips):
             copy1(a, lax.rem(me + k, chips), me).start()
         got[me, a] = chip[a, rows_of(me), :]
+
+    loads[0].wait()
+    loads[1].wait()
+    states_of(0, mine, other)
+    pl.semaphore_wait(barrier, chips + planes - 1)
+    copy0(0).start()
+    states_of(0, first, own)
+    loads[2].wait()
+    loads[3].wait()
+    states_of(1, mine, other)
+    copy0(1).start()
+    chip_sums(0)
+    states_of(1, first, own)
+    chip_sums(1)
 
     causal = (lax.broadcasted_iota(jnp.int32, (tokens, tokens), 1)
               <= lax.broadcasted_iota(jnp.int32, (tokens, tokens), 0))
@@ -164,6 +171,17 @@
 
     within(cut2, heads)
 
+    def finish(start, a):
+        for h in range(half):
+            cols = cols_of(start + h)
+            term = pre[a, cols, :]
+            if a == 0:
+                o_ref[:, cols] = (acc[0, :, cols] + dot(q_ref[:, cols], term, 1, 0)).astype(jnp.bfloat16)
+                gq_ref[:, cols] = (acc[1, :, cols] + dot(g_ref[:, cols], term, 1, 1)).astype(jnp.bfloat16)
+            else:
+                gk_ref[:, cols] = (acc[2, :, cols] + dot(v_ref[:, cols], term, 1, 1)).astype(jnp.bfloat16)
+                gv_ref[:, cols] = (acc[3, :, cols] + dot(k_ref[:, cols], term, 1, 0)).astype(jnp.bfloat16)
+
     my_rows = pl.ds(pl.multiple_of(core * half_rows, half_rows), half_rows)
     for a in range(2):
         for k in range(1, chips):
@@ -173,22 +191,11 @@
         later = core == (1 if a == 0 else 0)
         mate[a] = (base + jnp.where(later, 0.0, own[a])).astype(jnp.bfloat16)
         copy4(a, core).start()
-        pre[a, my_rows, :] = (base + jnp.where(later, paired[a].astype(jnp.float32), 0.0)).astype(jnp.bfloat16)
-
-    def finish(start):
-        for h in range(half):
-            cols = cols_of(start + h)
-            q, kk, v, g = q_ref[:, cols], k_ref[:, cols], v_ref[:, cols], g_ref[:, cols]
-            prefix, suffix = pre[0, cols, :], pre[1, cols, :]
-            o_ref[:, cols] = (acc[0, :, cols] + dot(q, prefix, 1, 0)).astype(jnp.bfloat16)
-            gq_ref[:, cols] = (acc[1, :, cols] + dot(g, prefix, 1, 1)).astype(jnp.bfloat16)
-            gk_ref[:, cols] = (acc[2, :, cols] + dot(v, suffix, 1, 1)).astype(jnp.bfloat16)
-            gv_ref[:, cols] = (acc[3, :, cols] + dot(kk, suffix, 1, 0)).astype(jnp.bfloat16)
-
-    finish(first)
+        pre[a, my_rows, :] = (base + jnp.where(later, paired[a], 0.0)).astype(jnp.bfloat16)
+        finish(first, a)
     for a in range(2):
         copy4(a, 1 - core).wait_recv()
-    finish(mine)
+        finish(mine, a)
 
     for a in range(2):
         copy0(a).wait_send()

time: 24 us -> 23.4 us (0.975)
  Pallas kernels: 23.2 us -> 22.6 us
    pallas_call x1, Pallas kernels: 21.9 us -> 21.2 us  [per_device(): pl.pallas_call(functools.partial(states_kernel, nh, ns, nx), out_shape=sh...]
where the time goes in v3:
time: 23.4 us; the launch traced here: 23.2 us
  Pallas kernels  22.6 us (97%)
  between operations  0.64 us (3%)
    pallas_call x1, Pallas kernels, per_device(): pl.pallas_call(functools.partial(states_kernel, nh, ns, nx), out_shape=sh...  21.2 us
    pallas_call x1, Pallas kernels, per_device(): pl.pallas_call(store_kernel, out_shape=shape, in_specs=[vmem] * 4, out_sp...  1.35 us

profile of v3, /device:TPU:1, one launch (start us, length us, event | category | flops | bytes accessed | tf_op | source)
XLA Modules:
  0.0 23.2 jit_solution(6270307844418917961)
XLA Ops:
  0.6 21.2 %shard_map.75 = (bf16[256,1024]{1,0:T(8,128)(2,1)S(1)}, bf16[256,1024]{1,0:T(8,128)(2,1)S(1)}, bf16[256,1024]{1,0:T(8,128)(2,1)S(1)}, bf16[256,1024]{1,0:T(8,128)(2,1)S(1)}) custom-call(bf16[256,1024]{1,0:T(8,128)(2,1)} %q_hbm.1, bf16[256,1024]{1,0:T(8,128)(2,1)} %k_hbm.1, bf16[256,1024]{1,0:T(8,128)(2,1)} %v_hbm.1, bf16[256,1024]{1,0:T(8,128)(2,1)} %g_hbm.1), custom_call_target="tpu_custom_call" | custom-call | flops 939524096 | bytes 4194304 | tf_op jit(solution)/shard_map/pallas_call | solution.py:234
  21.9 1.3 %shard_map.76 = (bf16[256,1024]{1,0:T(8,128)(2,1)}, bf16[256,1024]{1,0:T(8,128)(2,1)}, bf16[256,1024]{1,0:T(8,128)(2,1)}, bf16[256,1024]{1,0:T(8,128)(2,1)}) custom-call(bf16[256,1024]{1,0:T(8,128)(2,1)S(1)} %get-tuple-element.8.refs_0_, bf16[256,1024]{1,0:T(8,128)(2,1)S(1)} %get-tuple-element.9.refs_1_, bf16[256,1024]{1,0:T(8,128)(2,1)S(1)} %get-tuple-element.10.refs_2_, ...), custom_call_target="tpu_custom_call" | custom-call | bytes 4194304 | tf_op jit(solution)/shard_map/pallas_call | solution.py:261

commit v4 on v3

--- a/solution.py
+++ b/solution.py
@@ -35,6 +35,11 @@
     first, mine = core * half, (1 - core) * half
     partner = {"head": head_at + 1 - 2 * core, "seq": seq_at}
 
+    steps = [(dx, dy) for dx in range(nx) for dy in range(along) if dx or dy]
+    steps.sort(key=lambda step: -sum(d > 0 for d in step))
+    far_first = [lax.rem(me // along + dx, nx) * along + lax.rem(lax.rem(me, along) + dy, along)
+                 for dx, dy in steps]
+
     def in_plane(p):
         return {"head": lax.rem(p, along) * CORES + core, "seq": z * nx + p // along}
 
@@ -97,8 +102,8 @@
     def chip_sums(a):
         copy0(a).wait_recv()
         chip[a] = (own[a] + paired[a]).astype(chip.dtype)
-        for k in range(1, chips):
-            copy1(a, lax.rem(me + k, chips), me).start()
+        for there in far_first:
+            copy1(a, there, me).start()
         got[me, a] = chip[a, rows_of(me), :]
 
     loads[0].wait()
@@ -165,8 +170,8 @@
         for p in order:
             back[p, a] = run.astype(jnp.bfloat16)
             run = run + got[p, a].astype(jnp.float32)
-        for k in range(1, chips):
-            copy3(a, lax.rem(me + k, chips), me).start()
+        for there in far_first:
+            copy3(a, there, me).start()
         chippre[a, rows_of(me), :] = back[me, a]
 
     within(cut2, heads)

time: 23.4 us -> 23.2 us (level)
  no operation moved by 1% of the time
where the time goes in v4:
time: 23.2 us; the launch traced here: 23.1 us
  Pallas kernels  22.4 us (97%)
  between operations  0.64 us (3%)
    pallas_call x1, Pallas kernels, per_device(): pl.pallas_call(functools.partial(states_kernel, nh, ns, nx), out_shape=sh...  21.1 us
    pallas_call x1, Pallas kernels, per_device(): pl.pallas_call(store_kernel, out_shape=shape, in_specs=[vmem] * 4, out_sp...  1.35 us

profile of v4, /device:TPU:1, one launch (start us, length us, event | category | flops | bytes accessed | tf_op | source)
XLA Modules:
  0.0 23.1 jit_solution(1038377217105234488)
XLA Ops:
  0.6 21.1 %shard_map.75 = (bf16[256,1024]{1,0:T(8,128)(2,1)S(1)}, bf16[256,1024]{1,0:T(8,128)(2,1)S(1)}, bf16[256,1024]{1,0:T(8,128)(2,1)S(1)}, bf16[256,1024]{1,0:T(8,128)(2,1)S(1)}) custom-call(bf16[256,1024]{1,0:T(8,128)(2,1)} %q_hbm.1, bf16[256,1024]{1,0:T(8,128)(2,1)} %k_hbm.1, bf16[256,1024]{1,0:T(8,128)(2,1)} %v_hbm.1, bf16[256,1024]{1,0:T(8,128)(2,1)} %g_hbm.1), custom_call_target="tpu_custom_call" | custom-call | flops 939524096 | bytes 4194304 | tf_op jit(solution)/shard_map/pallas_call | solution.py:239
  21.7 1.3 %shard_map.76 = (bf16[256,1024]{1,0:T(8,128)(2,1)}, bf16[256,1024]{1,0:T(8,128)(2,1)}, bf16[256,1024]{1,0:T(8,128)(2,1)}, bf16[256,1024]{1,0:T(8,128)(2,1)}) custom-call(bf16[256,1024]{1,0:T(8,128)(2,1)S(1)} %get-tuple-element.8.refs_0_, bf16[256,1024]{1,0:T(8,128)(2,1)S(1)} %get-tuple-element.9.refs_1_, bf16[256,1024]{1,0:T(8,128)(2,1)S(1)} %get-tuple-element.10.refs_2_, ...), custom_call_target="tpu_custom_call" | custom-call | bytes 4194304 | tf_op jit(solution)/shard_map/pallas_call | solution.py:266
